TPU v7x, 256 devices: a whole 4x4x8 slice. The times are simulated.
256 devices in a mesh: dp: 8 (over z), ctx: 32 (over y, x, core).
Axes of the slice: x: 4, y: 4, z: 8, core: 2. Of those that a mesh axis runs over, the one named last changes fastest.
Arguments:
- output_gate_input: bfloat16 [8, 4096, 4096], P('dp', 'ctx'), may hold values from -6 to 6
- key_input: bfloat16 [8, 4096, 4096], P('dp', 'ctx'), may hold values from -6 to 6
- value_input: bfloat16 [8, 4096, 4096], P('dp', 'ctx'), may hold values from -6 to 6
- upstream: bfloat16 [8, 4096, 4096], P('dp', 'ctx'), may hold values from -6 to 6
- filter_taps: float32 [256, 4096], P('ctx'), may hold values from -6 to 6
- block_of_shard: int32 [32], replicated, may hold values from 0 to 31, each once
Outputs:
- mixed_out: bfloat16 [8, 4096, 4096], P('dp', 'ctx')
- gate_grad: bfloat16 [8, 4096, 4096], P('dp', 'ctx')
- key_grad: bfloat16 [8, 4096, 4096], P('dp', 'ctx')
- value_grad: bfloat16 [8, 4096, 4096], P('dp', 'ctx')
- taps_grad: float32 [256, 4096], P('ctx')
Inputs may be any that keep to these rules, and one draw needn't show every extreme that they name: block_of_shard names every block of positions exactly once.
All inputs are finite; a program needn't handle non-finite values.
Results may differ from a plain program's by a relative error of at most 0.012.
Values may be sent and summed in bfloat16 or wider, within the bound.
No kernel may reach another device: no remote copies, remote signals or barrier semaphores. Data moves between devices by JAX's collectives and lax.ppermute only.
A program may use at most 192 MiB of HBM per device.

v0:
```python
import math
import jax
import jax.numpy as jnp
from jax import lax
from jax.sharding import PartitionSpec as P

epsilon = 1e-06


def inverse_order(block_of_shard):
    pieces = block_of_shard.shape[0]
    labels = jnp.arange(pieces, dtype=jnp.int32)
    matches = (block_of_shard[:, None] == labels[None, :]).astype(jnp.int32)
    return jnp.sum(labels[:, None] * matches, axis=0)


def reorder_blocks(row_data, placing):
    pieces = placing.shape[0]
    shaped = row_data.reshape((pieces, row_data.shape[0] // pieces) + row_data.shape[1:])
    return jnp.take(shaped, placing, axis=0).reshape(row_data.shape)


def toeplitz_tables(kernel, block_rows):
    groups, length = kernel.shape
    pieces = length // block_rows
    padded = jnp.concatenate([jnp.zeros((groups, block_rows), kernel.dtype), kernel], axis=1)
    padded = padded.reshape(groups, pieces + 1, block_rows)
    tables = []
    for lag_block in range(pieces):
        segment = jnp.concatenate([padded[:, lag_block], padded[:, lag_block + 1]], axis=1)
        turned = jnp.roll(segment[:, ::-1], -(block_rows - 1), axis=1)
        flat = jnp.tile(turned, (1, block_rows))[:, : block_rows * (2 * block_rows - 1)]
        tables.append(flat.reshape(groups, block_rows, 2 * block_rows - 1)[:, :, :block_rows])
    return tables


def diagonal_sums(square):
    groups, block_rows, _ = square.shape
    flipped = square[:, :, ::-1]
    padded = jnp.pad(flipped, ((0, 0), (0, 0), (0, block_rows + 1)))
    flat = padded.reshape(groups, block_rows * (2 * block_rows + 1))[
        :, : 2 * block_rows * block_rows
    ]
    return jnp.sum(flat.reshape(groups, block_rows, 2 * block_rows), axis=1)


def forward_part(tables, signal, groups, block_rows):
    length, channels = signal.shape
    pieces = length // block_rows
    blocks = signal.reshape(pieces, block_rows, groups, channels // groups)
    total = jnp.zeros(blocks.shape, jnp.float32)
    for lag_block in range(pieces):
        contrib = jnp.einsum(
            "grs,jsgc->jrgc",
            tables[lag_block],
            blocks[: pieces - lag_block],
            preferred_element_type=jnp.float32,
        )
        total = total + jnp.pad(contrib, ((lag_block, 0), (0, 0), (0, 0), (0, 0)))
    return total.reshape(length, channels).astype(jnp.bfloat16)


def backward_part(tables, signal, weighted_seq, groups, block_rows):
    length, channels = signal.shape
    pieces = length // block_rows
    blocks = signal.reshape(pieces, block_rows, groups, channels // groups)
    wblocks = weighted_seq.reshape(pieces, block_rows, groups, channels // groups)
    total = jnp.zeros(blocks.shape, jnp.float32)
    lag_buffer = jnp.zeros((groups, (pieces + 1) * block_rows), jnp.float32)
    for lag_block in range(pieces):
        later = wblocks[lag_block:]
        contrib = jnp.einsum(
            "grs,jrgc->jsgc", tables[lag_block], later, preferred_element_type=jnp.float32
        )
        total = total + jnp.pad(contrib, ((0, lag_block), (0, 0), (0, 0), (0, 0)))
        square = jnp.einsum(
            "jrgc,jsgc->grs",
            later,
            blocks[: pieces - lag_block],
            preferred_element_type=jnp.float32,
        )
        folded = diagonal_sums(square)[:, : 2 * block_rows - 1]
        start = lag_block * block_rows + 1
        lag_buffer = lag_buffer + jnp.pad(
            folded, ((0, 0), (start, (pieces + 1) * block_rows - start - 2 * block_rows + 1))
        )
    returned = total.reshape(length, channels).astype(jnp.bfloat16)
    return (returned, lag_buffer[:, block_rows : block_rows + length])


def gate_product(first, second):
    return (first.astype(jnp.float32) * second.astype(jnp.float32)).astype(jnp.bfloat16)


def shards(output_gate_input, key_input, value_input, upstream, filter_taps, block_of_shard):
    inverse = inverse_order(block_of_shard)
    groups, length = filter_taps.shape
    block_rows = min(length, max(256, length // 16))
    root_mean = jnp.sqrt(jnp.mean(filter_taps * filter_taps, axis=1, keepdims=True) + epsilon)
    norm_scale = 1.0 / (math.sqrt(length) * root_mean)
    kernel = (filter_taps * norm_scale).astype(jnp.bfloat16)
    tables = toeplitz_tables(kernel, block_rows)
    gates_here = output_gate_input[0]
    keys_here = key_input[0]
    values_here = value_input[0]
    upstream_here = upstream[0]
    product = gate_product(keys_here, values_here)
    arrived = (
        lax.all_to_all(product, "ctx", split_axis=1, concat_axis=0, tiled=True),
        lax.all_to_all(gates_here, "ctx", split_axis=1, concat_axis=0, tiled=True),
        lax.all_to_all(upstream_here, "ctx", split_axis=1, concat_axis=0, tiled=True),
    )
    signal = reorder_blocks(arrived[0], inverse)
    gates_seq = reorder_blocks(arrived[1], inverse)
    upstream_seq = reorder_blocks(arrived[2], inverse)
    mixing = forward_part(tables, signal, groups, block_rows)
    weighted_seq = gate_product(upstream_seq, gates_seq)
    returned, lag_sums = backward_part(tables, signal, weighted_seq, groups, block_rows)
    mixed_seq = reorder_blocks(gate_product(gates_seq, mixing), block_of_shard)
    gate_seq = reorder_blocks(gate_product(upstream_seq, mixing), block_of_shard)
    returned = reorder_blocks(returned, block_of_shard)
    mixed_out, gate_grad, returned_here = (
        lax.all_to_all(mixed_seq, "ctx", split_axis=0, concat_axis=1, tiled=True),
        lax.all_to_all(gate_seq, "ctx", split_axis=0, concat_axis=1, tiled=True),
        lax.all_to_all(returned, "ctx", split_axis=0, concat_axis=1, tiled=True),
    )
    key_grad = gate_product(returned_here, values_here)
    value_grad = gate_product(returned_here, keys_here)
    lag_total = lax.psum(lag_sums, "dp")
    lag_mean = lag_total / lax.axis_size("dp")
    projection = jnp.sum(lag_mean * filter_taps, axis=1, keepdims=True)
    taps_grad = (
        norm_scale * lag_mean - filter_taps * (norm_scale * norm_scale * norm_scale) * projection
    )
    return (mixed_out[None], gate_grad[None], key_grad[None], value_grad[None], taps_grad)


def solution(mesh):
    return jax.shard_map(
        shards,
        mesh=mesh,
        in_specs=(
            P("dp", "ctx", None),
            P("dp", "ctx", None),
            P("dp", "ctx", None),
            P("dp", "ctx", None),
            P("ctx", None),
            P(),
        ),
        out_specs=(
            P("dp", "ctx", None),
            P("dp", "ctx", None),
            P("dp", "ctx", None),
            P("dp", "ctx", None),
            P("ctx", None),
        ),
        check_vma=False,
    )
```

profile of v0, /device:TPU:1, one launch (start us, length us, event | category | flops | bytes accessed | tf_op | source)
XLA Modules:
  0.0 1130.7 jit_solution(15635006254996681494)
XLA Ops:
  11.2 8.7 all-to-all-start.1
  21.9 15.2 %all-to-all-done.1 = bf16[128,32,128]{2,0,1:T(8,128)(2,1)S(1)} async-done(((bf16[128,32,128]{2,0,1:T(8,128)(2,1)}), bf16[128,32,128]{2,0,1:T(8,128)(2,1)S(1)}, u32[]{:S(2)}, u32[]{:S(2)}) %all-to-all-start.1) | async-done | bytes 1048608 | tf_op jit(solution)/shard_map/all_to_all | solution.py:109
  44.1 14.2 %all-to-all-done = bf16[128,32,128]{2,0,1:T(8,128)(2,1)S(1)} async-done(((bf16[128,32,128]{2,0,1:T(8,128)(2,1)}), bf16[128,32,128]{2,0,1:T(8,128)(2,1)S(1)}, u32[]{:S(2)}, u32[]{:S(2)}) %all-to-all-start) | async-done | bytes 1048608 | tf_op jit(solution)/shard_map/all_to_all | solution.py:110
  58.4 4.7 all-to-all-start.3
  68.2 12.2 %all-to-all-done.3 = bf16[128,32,128]{2,0,1:T(8,128)(2,1)} async-done(((bf16[128,32,128]{2,0,1:T(8,128)(2,1)}), bf16[128,32,128]{2,0,1:T(8,128)(2,1)}, u32[]{:S(2)}, u32[]{:S(2)}) %all-to-all-start.3) | async-done | bytes 1048608 | tf_op jit(solution)/shard_map/all_to_all | solution.py:111
  151.3 17.5 %rev.65 = f32[8,256,256]{2,1,0:T(8,128)} reverse(f32[8,256,256]{2,1,0:T(8,128)} %convolution_bitcast_fusion.10), dimensions={2} | reverse | bytes 4194304 | tf_op jit(solution)/shard_map/rev | solution.py:39
  170.7 17.7 %rev.64 = f32[8,256,256]{2,1,0:T(8,128)} reverse(f32[8,256,256]{2,1,0:T(8,128)} %convolution_bitcast_fusion.11), dimensions={2} | reverse | bytes 4194304 | tf_op jit(solution)/shard_map/rev | solution.py:39
  190.2 17.7 %rev.66 = f32[8,256,256]{2,1,0:T(8,128)} reverse(f32[8,256,256]{2,1,0:T(8,128)} %convolution_bitcast_fusion.9), dimensions={2} | reverse | bytes 4194304 | tf_op jit(solution)/shard_map/rev | solution.py:39
  209.7 17.7 %rev.67 = f32[8,256,256]{2,1,0:T(8,128)} reverse(f32[8,256,256]{2,1,0:T(8,128)} %convolution_bitcast_fusion.8), dimensions={2} | reverse | bytes 4194304 | tf_op jit(solution)/shard_map/rev | solution.py:39
  229.2 17.7 %rev.68 = f32[8,256,256]{2,1,0:T(8,128)} reverse(f32[8,256,256]{2,1,0:T(8,128)} %convolution_bitcast_fusion.7), dimensions={2} | reverse | bytes 4194304 | tf_op jit(solution)/shard_map/rev | solution.py:39
  248.6 17.7 %rev.69 = f32[8,256,256]{2,1,0:T(8,128)} reverse(f32[8,256,256]{2,1,0:T(8,128)} %convolution_bitcast_fusion.6), dimensions={2} | reverse | bytes 4194304 | tf_op jit(solution)/shard_map/rev | solution.py:39
  268.2 17.7 %rev.70 = f32[8,256,256]{2,1,0:T(8,128)} reverse(f32[8,256,256]{2,1,0:T(8,128)} %convolution_bitcast_fusion.5), dimensions={2} | reverse | bytes 4194304 | tf_op jit(solution)/shard_map/rev | solution.py:39
  287.7 17.6 %rev.71 = f32[8,256,256]{2,1,0:T(8,128)} reverse(f32[8,256,256]{2,1,0:T(8,128)} %convolution_bitcast_fusion.4), dimensions={2} | reverse | bytes 4194304 | tf_op jit(solution)/shard_map/rev | solution.py:39
  305.8 11.6 %rev.72 = f32[8,256,256]{2,1,0:T(8,128)} reverse(f32[8,256,256]{2,1,0:T(8,128)S(1)} %convolution_bitcast_fusion.14), dimensions={2} | reverse | bytes 4194304 | tf_op jit(solution)/shard_map/rev | solution.py:39
  319.1 11.6 %rev.73 = f32[8,256,256]{2,1,0:T(8,128)} reverse(f32[8,256,256]{2,1,0:T(8,128)S(1)} %convolution_bitcast_fusion.3), dimensions={2} | reverse | bytes 4194304 | tf_op jit(solution)/shard_map/rev | solution.py:39
  331.2 11.6 %rev.74 = f32[8,256,256]{2,1,0:T(8,128)} reverse(f32[8,256,256]{2,1,0:T(8,128)S(1)} %convolution_bitcast_fusion.2), dimensions={2} | reverse | bytes 4194304 | tf_op jit(solution)/shard_map/rev | solution.py:39
  343.3 11.6 %rev.75 = f32[8,256,256]{2,1,0:T(8,128)} reverse(f32[8,256,256]{2,1,0:T(8,128)S(1)} %convolution_bitcast_fusion.1), dimensions={2} | reverse | bytes 4194304 | tf_op jit(solution)/shard_map/rev | solution.py:39
  355.4 11.6 %rev.76 = f32[8,256,256]{2,1,0:T(8,128)} reverse(f32[8,256,256]{2,1,0:T(8,128)S(1)} %convolution_bitcast_fusion.13), dimensions={2} | reverse | bytes 4194304 | tf_op jit(solution)/shard_map/rev | solution.py:39
  367.5 11.6 %rev.77 = f32[8,256,256]{2,1,0:T(8,128)} reverse(f32[8,256,256]{2,1,0:T(8,128)S(1)} %convolution_bitcast_fusion.12), dimensions={2} | reverse | bytes 4194304 | tf_op jit(solution)/shard_map/rev | solution.py:39
  379.6 11.6 %rev.78 = f32[8,256,256]{2,1,0:T(8,128)} reverse(f32[8,256,256]{2,1,0:T(8,128)S(1)} %convolution_bitcast_fusion), dimensions={2} | reverse | bytes 4194304 | tf_op jit(solution)/shard_map/rev | solution.py:39
  391.7 11.8 %rev.79 = f32[8,256,256]{2,1,0:T(8,128)} reverse(f32[8,256,256]{2,1,0:T(8,128)S(1)} %fusion.81), dimensions={2} | reverse | bytes 4194304 | tf_op jit(solution)/shard_map/rev | solution.py:39
  407.8 7.1 reshape.447
  424.9 7.1 reshape.445
  432.0 4.5 slice.1016
  442.0 7.1 reshape.443
  449.1 4.5 slice.1014
  459.2 7.3 reshape.441
  476.5 7.1 reshape.439
  483.5 4.5 slice.1010
  493.6 7.1 reshape.437
  500.7 4.5 slice.1008
  510.7 7.5 reshape.435
  518.2 4.5 slice.1006
  528.2 7.1 reshape.433
  545.4 7.1 reshape.431
  562.5 7.1 reshape.429
  579.7 7.1 reshape.427
  596.9 7.1 reshape.425
  614.0 7.1 reshape.423
  631.1 7.3 reshape.421
  648.4 7.1 reshape.417
  665.5 7.1 reshape.419
  681.1 65.4 %all-reduce.65.cloned.1.call-done = f32[8,4096]{1,0:T(8,128)} async-done(((f32[8,4096]{1,0:T(8,128)}), f32[8,4096]{1,0:T(8,128)}) %all-reduce.65.cloned.1.call-update) | async-done | bytes 131088 | tf_op jit(solution)/shard_map/psum | solution.py:129
  764.5 5.1 reshape.407
  777.8 5.3 reshape.406
  791.4 5.1 reshape.405
  804.9 5.2 reshape.404
  820.7 5.0 reshape.403
  838.0 5.0 reshape.402
  855.1 5.2 reshape.401
  872.4 5.0 reshape.400
  889.7 5.2 reshape.415
  905.8 5.0 reshape.413
  922.0 5.4 reshape.412
  938.8 5.0 reshape.411
  955.3 5.2 reshape.410
  971.3 5.0 reshape.409
  986.0 5.2 reshape.408
  1000.3 5.0 reshape.399
  1005.3 7.7 fusion.36
  1025.2 5.8 fusion.35
  1041.0 29.5 %all_to_all.81 = bf16[32,128,128]{2,1,0:T(8,128)(2,1)S(1)} all-to-all(bf16[32,128,128]{2,1,0:T(8,128)(2,1)S(1)} %get-tuple-element.60), channel_id=1, replica_groups=mesh['dp'=8,'ctx'=32] {'ctx'}, dimensions={0} | all-to-all | bytes 2097152 | tf_op jit(solution)/shard_map/all_to_all | solution.py:124
  1070.5 20.7 %all_to_all.82 = bf16[32,128,128]{2,1,0:T(8,128)(2,1)S(1)} all-to-all(bf16[32,128,128]{2,1,0:T(8,128)(2,1)S(1)} %get-tuple-element.61), channel_id=1, replica_groups=mesh['dp'=8,'ctx'=32] {'ctx'}, dimensions={0} | all-to-all | bytes 2097152 | tf_op jit(solution)/shard_map/all_to_all | solution.py:123
  1100.7 11.7 %all-to-all-done.5 = bf16[32,128,128]{2,1,0:T(8,128)(2,1)S(1)} async-done(((bf16[32,128,128]{2,1,0:T(8,128)(2,1)}), bf16[32,128,128]{2,1,0:T(8,128)(2,1)S(1)}, u32[]{:S(2)}, u32[]{:S(2)}) %all-to-all-start.5) | async-done | bytes 1048608 | tf_op jit(solution)/shard_map/all_to_all | solution.py:125
  (579 shorter events, 467.0 us)
Async XLA Ops:
  11.2 8.7 copy-start.74
  11.2 25.9 %all-to-all-start.1 = ((bf16[128,32,128]{2,0,1:T(8,128)(2,1)}), bf16[128,32,128]{2,0,1:T(8,128)(2,1)S(1)}, u32[]{:S(2)}, u32[]{:S(2)}) async-start(bf16[128,32,128]{2,0,1:T(8,128)(2,1)} %copy.207), calls=%async_computation.1 | async-start | bytes 2097152 | tf_op jit(solution)/shard_map/all_to_all | solution.py:109
  37.1 21.3 %all-to-all-start = ((bf16[128,32,128]{2,0,1:T(8,128)(2,1)}), bf16[128,32,128]{2,0,1:T(8,128)(2,1)S(1)}, u32[]{:S(2)}, u32[]{:S(2)}) async-start(bf16[128,32,128]{2,0,1:T(8,128)(2,1)} %copy.204), calls=%async_computation | async-start | bytes 2097152 | tf_op jit(solution)/shard_map/all_to_all | solution.py:110
  58.4 22.0 %all-to-all-start.3 = ((bf16[128,32,128]{2,0,1:T(8,128)(2,1)}), bf16[128,32,128]{2,0,1:T(8,128)(2,1)}, u32[]{:S(2)}, u32[]{:S(2)}) async-start(bf16[128,32,128]{2,0,1:T(8,128)(2,1)} %copy.243), calls=%async_computation.3 | async-start | bytes 2097152 | tf_op jit(solution)/shard_map/all_to_all | solution.py:111
  63.0 683.4 %all-reduce.65.cloned.1.call-start = ((), (), s32[]{:S(2)}) async-start(), calls=%async_computation.6 | async-start | bytes 262144 | tf_op jit(solution)/shard_map/psum | solution.py:129
  63.3 19.1 %copy-start.79 = (pred[32]{0:T(512)(128)(4,1)}, pred[32]{0:T(512)(128)(4,1)S(1)}, u32[]{:S(2)}) copy-start(pred[32]{0:T(512)(128)(4,1)S(1)} %compare_and_fusion.1) | copy-start | bytes 100
  68.2 14.8 %copy-start.2 = (bf16[32,128,128]{2,1,0:T(8,128)(2,1)}, bf16[32,128,128]{2,1,0:T(8,128)(2,1)S(1)}, u32[]{:S(2)}) copy-start(bf16[32,128,128]{2,1,0:T(8,128)(2,1)S(1)} %gather_fusion) | copy-start | bytes 3145732
  83.9 4.3 slice-start.4
  85.8 305.4 %copy-start.75 = (bf16[256,8,16]{0,2,1:T(8,128)(2,1)}, bf16[256,8,16]{0,2,1:T(8,128)(2,1)S(1)}, u32[]{:S(2)}) copy-start(bf16[256,8,16]{0,2,1:T(8,128)(2,1)S(1)} %reshape.414) | copy-start | bytes 196612
  86.0 3.6 slice-start.5
  87.1 279.9 %copy-start.60 = (bf16[3,256,8,16]{1,0,3,2:T(4,128)(2,1)}, bf16[3,256,8,16]{1,0,3,2:T(4,128)(2,1)S(1)}, u32[]{:S(2)}) copy-start(bf16[3,256,8,16]{1,0,3,2:T(4,128)(2,1)S(1)} %slice.794) | copy-start | bytes 589828
  87.4 3.7 slice-start.6
  106.0 62.8 %copy-start.31 = (bf16[16,256,8,16]{1,0,3,2:T(8,128)(2,1)}, bf16[16,256,8,16]{1,0,3,2:T(8,128)(2,1)S(1)}, u32[]{:S(2)}) copy-start(bf16[16,256,8,16]{1,0,3,2:T(8,128)(2,1)S(1)} %reshape_reshape.4) | copy-start | bytes 3145732
  106.0 4.7 slice-start.15
  106.1 5.5 slice-start.16
  106.1 6.4 slice-start.17
  108.0 5.5 slice-start.18
  108.0 6.6 slice-start.19
  111.7 4.4 slice-start.20
  113.7 3.7 slice-start.21
  116.0 4.6 slice-start.22
  117.4 4.6 slice-start.23
  121.1 4.4 slice-start.24
  123.3 3.9 slice-start.25
  130.6 3.5 slice-start.27
  134.1 4.2 slice-start.28
  140.1 3.7 slice-start.29
  143.8 25.1 %copy-start.32 = (bf16[16,256,8,16]{1,0,3,2:T(8,128)(2,1)}, bf16[16,256,8,16]{1,0,3,2:T(8,128)(2,1)S(1)}, u32[]{:S(2)}) copy-start(bf16[16,256,8,16]{1,0,3,2:T(8,128)(2,1)S(1)} %convert_element_type.227) | copy-start | bytes 3145732
  170.7 17.7 %copy-start.35 = (bf16[14,256,8,16]{1,0,3,2:T(8,128)(2,1)S(1)}, bf16[14,256,8,16]{1,0,3,2:T(8,128)(2,1)}, u32[]{:S(2)}) copy-start(bf16[14,256,8,16]{1,0,3,2:T(8,128)(2,1)} %slice.695) | copy-start | bytes 2752516
  170.7 17.7 %copy-start.37 = (bf16[14,256,8,16]{1,0,3,2:T(8,128)(2,1)S(1)}, bf16[14,256,8,16]{1,0,3,2:T(8,128)(2,1)}, u32[]{:S(2)}) copy-start(bf16[14,256,8,16]{1,0,3,2:T(8,128)(2,1)} %slice.822) | copy-start | bytes 2752516
  190.2 17.7 %copy-start.38 = (bf16[13,256,8,16]{1,0,3,2:T(8,128)(2,1)S(1)}, bf16[13,256,8,16]{1,0,3,2:T(8,128)(2,1)}, u32[]{:S(2)}) copy-start(bf16[13,256,8,16]{1,0,3,2:T(8,128)(2,1)} %slice.704) | copy-start | bytes 2555908
  190.2 17.7 %copy-start.40 = (bf16[13,256,8,16]{1,0,3,2:T(8,128)(2,1)S(1)}, bf16[13,256,8,16]{1,0,3,2:T(8,128)(2,1)}, u32[]{:S(2)}) copy-start(bf16[13,256,8,16]{1,0,3,2:T(8,128)(2,1)} %slice.824) | copy-start | bytes 2555908
  209.7 17.7 %copy-start.41 = (bf16[12,256,8,16]{1,0,3,2:T(8,128)(2,1)S(1)}, bf16[12,256,8,16]{1,0,3,2:T(8,128)(2,1)}, u32[]{:S(2)}) copy-start(bf16[12,256,8,16]{1,0,3,2:T(8,128)(2,1)} %slice.713) | copy-start | bytes 2359300
  209.7 17.7 %copy-start.43 = (bf16[12,256,8,16]{1,0,3,2:T(8,128)(2,1)S(1)}, bf16[12,256,8,16]{1,0,3,2:T(8,128)(2,1)}, u32[]{:S(2)}) copy-start(bf16[12,256,8,16]{1,0,3,2:T(8,128)(2,1)} %slice.826) | copy-start | bytes 2359300
  229.2 17.7 %copy-start.44 = (bf16[11,256,8,16]{1,0,3,2:T(8,128)(2,1)S(1)}, bf16[11,256,8,16]{1,0,3,2:T(8,128)(2,1)}, u32[]{:S(2)}) copy-start(bf16[11,256,8,16]{1,0,3,2:T(8,128)(2,1)} %slice.722) | copy-start | bytes 2162692
  229.2 17.7 %copy-start.46 = (bf16[11,256,8,16]{1,0,3,2:T(8,128)(2,1)S(1)}, bf16[11,256,8,16]{1,0,3,2:T(8,128)(2,1)}, u32[]{:S(2)}) copy-start(bf16[11,256,8,16]{1,0,3,2:T(8,128)(2,1)} %slice.828) | copy-start | bytes 2162692
  248.6 17.7 %copy-start.47 = (bf16[10,256,8,16]{1,0,3,2:T(8,128)(2,1)S(1)}, bf16[10,256,8,16]{1,0,3,2:T(8,128)(2,1)}, u32[]{:S(2)}) copy-start(bf16[10,256,8,16]{1,0,3,2:T(8,128)(2,1)} %slice.731) | copy-start | bytes 1966084
  248.6 17.7 %copy-start.49 = (bf16[10,256,8,16]{1,0,3,2:T(8,128)(2,1)S(1)}, bf16[10,256,8,16]{1,0,3,2:T(8,128)(2,1)}, u32[]{:S(2)}) copy-start(bf16[10,256,8,16]{1,0,3,2:T(8,128)(2,1)} %slice.830) | copy-start | bytes 1966084
  268.1 17.7 %copy-start.51 = (bf16[9,256,8,16]{1,0,3,2:T(8,128)(2,1)S(1)}, bf16[9,256,8,16]{1,0,3,2:T(8,128)(2,1)}, u32[]{:S(2)}) copy-start(bf16[9,256,8,16]{1,0,3,2:T(8,128)(2,1)} %slice.740) | copy-start | bytes 1769476
  268.1 17.7 %copy-start.53 = (bf16[9,256,8,16]{1,0,3,2:T(8,128)(2,1)S(1)}, bf16[9,256,8,16]{1,0,3,2:T(8,128)(2,1)}, u32[]{:S(2)}) copy-start(bf16[9,256,8,16]{1,0,3,2:T(8,128)(2,1)} %slice.832) | copy-start | bytes 1769476
  287.7 17.6 %copy-start.55 = (bf16[8,256,8,16]{1,0,3,2:T(8,128)(2,1)S(1)}, bf16[8,256,8,16]{1,0,3,2:T(8,128)(2,1)}, u32[]{:S(2)}) copy-start(bf16[8,256,8,16]{1,0,3,2:T(8,128)(2,1)} %slice.749) | copy-start | bytes 1572868
  287.7 17.6 %copy-start.57 = (bf16[8,256,8,16]{1,0,3,2:T(8,128)(2,1)S(1)}, bf16[8,256,8,16]{1,0,3,2:T(8,128)(2,1)}, u32[]{:S(2)}) copy-start(bf16[8,256,8,16]{1,0,3,2:T(8,128)(2,1)} %slice.834) | copy-start | bytes 1572868
  319.0 11.7 %copy-start.62 = (bf16[6,256,8,16]{1,0,3,2:T(8,128)(2,1)S(1)}, bf16[6,256,8,16]{1,0,3,2:T(8,128)(2,1)}, u32[]{:S(2)}) copy-start(bf16[6,256,8,16]{1,0,3,2:T(8,128)(2,1)} %slice.767) | copy-start | bytes 1179652
  319.1 11.6 %copy-start.64 = (bf16[6,256,8,16]{1,0,3,2:T(8,128)(2,1)S(1)}, bf16[6,256,8,16]{1,0,3,2:T(8,128)(2,1)}, u32[]{:S(2)}) copy-start(bf16[6,256,8,16]{1,0,3,2:T(8,128)(2,1)} %slice.838) | copy-start | bytes 1179652
  331.2 11.6 %copy-start.66 = (bf16[5,256,8,16]{1,0,3,2:T(8,128)(2,1)S(1)}, bf16[5,256,8,16]{1,0,3,2:T(8,128)(2,1)}, u32[]{:S(2)}) copy-start(bf16[5,256,8,16]{1,0,3,2:T(8,128)(2,1)} %slice.776) | copy-start | bytes 983044
  331.2 11.6 %copy-start.68 = (bf16[5,256,8,16]{1,0,3,2:T(8,128)(2,1)S(1)}, bf16[5,256,8,16]{1,0,3,2:T(8,128)(2,1)}, u32[]{:S(2)}) copy-start(bf16[5,256,8,16]{1,0,3,2:T(8,128)(2,1)} %slice.840) | copy-start | bytes 983044
  343.3 11.6 %copy-start.71 = (bf16[4,256,8,16]{1,0,3,2:T(4,128)(2,1)S(1)}, bf16[4,256,8,16]{1,0,3,2:T(4,128)(2,1)}, u32[]{:S(2)}) copy-start(bf16[4,256,8,16]{1,0,3,2:T(4,128)(2,1)} %slice.785) | copy-start | bytes 786436
  343.3 11.6 %copy-start.72 = (bf16[4,256,8,16]{1,0,3,2:T(4,128)(2,1)S(1)}, bf16[4,256,8,16]{1,0,3,2:T(4,128)(2,1)}, u32[]{:S(2)}) copy-start(bf16[4,256,8,16]{1,0,3,2:T(4,128)(2,1)} %slice.842) | copy-start | bytes 786436
  355.4 11.6 %copy-start.61 = (bf16[3,256,8,16]{1,0,3,2:T(4,128)(2,1)S(1)}, bf16[3,256,8,16]{1,0,3,2:T(4,128)(2,1)}, u32[]{:S(2)}) copy-start(bf16[3,256,8,16]{1,0,3,2:T(4,128)(2,1)} %slice.844) | copy-start | bytes 589828
  367.5 11.6 %copy-start.69 = (bf16[2,256,8,16]{1,0,3,2:T(2,128)(2,1)S(1)}, bf16[2,256,8,16]{1,0,3,2:T(2,128)(2,1)}, u32[]{:S(2)}) copy-start(bf16[2,256,8,16]{1,0,3,2:T(2,128)(2,1)} %slice.803) | copy-start | bytes 393220
  367.5 11.6 %copy-start.70 = (bf16[2,256,8,16]{1,0,3,2:T(2,128)(2,1)S(1)}, bf16[2,256,8,16]{1,0,3,2:T(2,128)(2,1)}, u32[]{:S(2)}) copy-start(bf16[2,256,8,16]{1,0,3,2:T(2,128)(2,1)} %slice.846) | copy-start | bytes 393220
  379.6 11.6 %copy-start.76 = (bf16[256,8,16]{0,2,1:T(8,128)(2,1)S(1)}, bf16[256,8,16]{0,2,1:T(8,128)(2,1)}, u32[]{:S(2)}) copy-start(bf16[256,8,16]{0,2,1:T(8,128)(2,1)} %reshape.416) | copy-start | bytes 196612
  677.1 69.4 %copy-start.77 = (f32[8,4096]{1,0:T(8,128)S(1)}, f32[8,4096]{1,0:T(8,128)}, u32[]{:S(2)}) copy-start(f32[8,4096]{1,0:T(8,128)} %param.12) | copy-start | bytes 393220
  764.5 5.1 copy-start.58
  777.8 5.3 copy-start.54
  791.4 5.1 copy-start.50
  991.2 3.7 copy-start.78
  1005.3 7.7 copy-start.10
  1021.3 3.8 copy-start.11
  1021.4 3.8 copy-start.27
  1021.4 3.8 copy-start.28
  1021.4 3.8 copy-start.65
  1034.6 3.9 copy-start.81
  1091.2 21.3 %all-to-all-start.5 = ((bf16[32,128,128]{2,1,0:T(8,128)(2,1)}), bf16[32,128,128]{2,1,0:T(8,128)(2,1)S(1)}, u32[]{:S(2)}, u32[]{:S(2)}) async-start(bf16[32,128,128]{2,1,0:T(8,128)(2,1)} %get-tuple-element.59), calls=%async_computation.5 | async-start | bytes 2097152 | tf_op jit(solution)/shard_map/all_to_all | solution.py:125
  (55 other events, 136.3 us)
Sparse Core Ops, SparseCore 0:
  680.6 65.8 all-reduce.64
where the time goes:
time: 1150 us; the launch traced here: 1130 us
  local copies, waits for them, and re-layouts  770 us (67%)
  waiting for transfers between devices  119 us (10%)
  matrix products  92.7 us (8%)
  other arithmetic  61.6 us (5%)
  blocking collectives  50.2 us (4%)
  starting transfers between devices  21.5 us (2%)
  between operations  15.9 us (1%)
    rev x16, local copies, waits for them, and re-layouts, diagonal_sums(): flipped = square[:, :, ::-1]  234 us
    unnamed x256, local copies, waits for them, and re-layouts  117 us
    reshape x16, local copies, waits for them, and re-layouts, diagonal_sums(): padded.reshape(groups, block_rows * (2 * block_rows + 1))  114 us
    reshape x16, local copies, waits for them, and re-layouts, toeplitz_tables(): flat.reshape(groups, block_rows, 2 * block_rows - 1)[:, :, :block_rows]  81.9 us
    slice x16, local copies, waits for them, and re-layouts, diagonal_sums(): padded.reshape(groups, block_rows * (2 * block_rows + 1))  71.3 us
    psum x1, waiting for transfers between devices, shards(): lag_total = lax.psum(lag_sums, 'dp')  65.4 us
    pad x16, local copies, waits for them, and re-layouts, diagonal_sums(): padded = jnp.pad(flipped, ((0, 0), (0, 0), (0, block_rows + 1)))  45.8 us
    reduce_sum x16, other arithmetic, diagonal_sums(): return jnp.sum(flat.reshape(groups, block_rows, 2 * block_rows), axis=1)  42.4 us
  transfers between devices with their start and end apart: 5, of which 5 were waited for; matrix products, arithmetic and copies ran while one was open for 1% of the time, Pallas kernels for 0%

commit v1 on v0

--- a/solution.py
+++ b/solution.py
@@ -126,7 +126,11 @@
     )
     key_grad = gate_product(returned_here, values_here)
     value_grad = gate_product(returned_here, keys_here)
-    lag_total = lax.psum(lag_sums, "dp")
+    lag_total = lag_sums
+    for hop in (1, 2, 4):
+        lag_total = lag_total + lax.ppermute(
+            lag_total, "dp", [(dev, dev ^ hop) for dev in range(8)]
+        )
     lag_mean = lag_total / lax.axis_size("dp")
     projection = jnp.sum(lag_mean * filter_taps, axis=1, keepdims=True)
     taps_grad = (

time: 1150 us -> 1090 us (0.948)
  waiting for transfers between devices: 119 us -> 64.8 us
  between operations: 15.9 us -> 2.46 us
  starting transfers between devices: 21.5 us -> 33 us
    psum x1 -> x0, waiting for transfers between devices: 65.4 us -> none  [shards(): lag_total = lax.psum(lag_sums, 'dp')]
  transfers between devices with their start and end apart: 5 -> 7, of which waited for: 5 -> 7; matrix products, arithmetic and copies ran while one was open for 1% -> 1% of each run, Pallas kernels for 0% -> 0%
where the time goes in v1:
time: 1090 us; the launch traced here: 1070 us
  local copies, waits for them, and re-layouts  771 us (71%)
  matrix products  92.9 us (9%)
  waiting for transfers between devices  64.8 us (6%)
  other arithmetic  59.2 us (5%)
  blocking collectives  46.3 us (4%)
  starting transfers between devices  33 us (3%)
    rev x16, local copies, waits for them, and re-layouts, diagonal_sums(): flipped = square[:, :, ::-1]  235 us
    unnamed x256, local copies, waits for them, and re-layouts  118 us
    reshape x16, local copies, waits for them, and re-layouts, diagonal_sums(): padded.reshape(groups, block_rows * (2 * block_rows + 1))  113 us
    reshape x16, local copies, waits for them, and re-layouts, toeplitz_tables(): flat.reshape(groups, block_rows, 2 * block_rows - 1)[:, :, :block_rows]  81.9 us
    slice x16, local copies, waits for them, and re-layouts, diagonal_sums(): padded.reshape(groups, block_rows * (2 * block_rows + 1))  71.4 us
    pad x16, local copies, waits for them, and re-layouts, diagonal_sums(): padded = jnp.pad(flipped, ((0, 0), (0, 0), (0, block_rows + 1)))  46.1 us
    reduce_sum x16, other arithmetic, diagonal_sums(): return jnp.sum(flat.reshape(groups, block_rows, 2 * block_rows), axis=1)  42.4 us
    dot_general x16, matrix products, backward_part(): jnp.einsum('grs,jrgc->jsgc', tables[lag_block], later, preferred_element_...  38.4 us
  transfers between devices with their start and end apart: 7, of which 7 were waited for; matrix products, arithmetic and copies ran while one was open for 1% of the time, Pallas kernels for 0%

profile of v1, /device:TPU:1, one launch (start us, length us, event | category | flops | bytes accessed | tf_op | source)
XLA Modules:
  0.0 1069.8 jit_solution(4418385223171102422)
XLA Ops:
  4.7 8.7 all-to-all-start.1
  15.4 15.2 %all-to-all-done.1 = bf16[128,32,128]{2,0,1:T(8,128)(2,1)S(1)} async-done(((bf16[128,32,128]{2,0,1:T(8,128)(2,1)}), bf16[128,32,128]{2,0,1:T(8,128)(2,1)S(1)}, u32[]{:S(2)}, u32[]{:S(2)}) %all-to-all-start.1) | async-done | bytes 1048608 | tf_op jit(solution)/shard_map/all_to_all | solution.py:109
  37.5 14.3 %all-to-all-done = bf16[128,32,128]{2,0,1:T(8,128)(2,1)S(1)} async-done(((bf16[128,32,128]{2,0,1:T(8,128)(2,1)}), bf16[128,32,128]{2,0,1:T(8,128)(2,1)S(1)}, u32[]{:S(2)}, u32[]{:S(2)}) %all-to-all-start) | async-done | bytes 1048608 | tf_op jit(solution)/shard_map/all_to_all | solution.py:110
  51.9 5.0 all-to-all-start.3
  61.4 12.7 %all-to-all-done.3 = bf16[128,32,128]{2,0,1:T(8,128)(2,1)} async-done(((bf16[128,32,128]{2,0,1:T(8,128)(2,1)}), bf16[128,32,128]{2,0,1:T(8,128)(2,1)}, u32[]{:S(2)}, u32[]{:S(2)}) %all-to-all-start.3) | async-done | bytes 1048608 | tf_op jit(solution)/shard_map/all_to_all | solution.py:111
  145.1 17.5 %rev.65 = f32[8,256,256]{2,1,0:T(8,128)} reverse(f32[8,256,256]{2,1,0:T(8,128)} %convolution_bitcast_fusion.10), dimensions={2} | reverse | bytes 4194304 | tf_op jit(solution)/shard_map/rev | solution.py:39
  164.5 17.7 %rev.64 = f32[8,256,256]{2,1,0:T(8,128)} reverse(f32[8,256,256]{2,1,0:T(8,128)} %convolution_bitcast_fusion.11), dimensions={2} | reverse | bytes 4194304 | tf_op jit(solution)/shard_map/rev | solution.py:39
  184.0 17.7 %rev.66 = f32[8,256,256]{2,1,0:T(8,128)} reverse(f32[8,256,256]{2,1,0:T(8,128)} %convolution_bitcast_fusion.9), dimensions={2} | reverse | bytes 4194304 | tf_op jit(solution)/shard_map/rev | solution.py:39
  203.5 17.7 %rev.67 = f32[8,256,256]{2,1,0:T(8,128)} reverse(f32[8,256,256]{2,1,0:T(8,128)} %convolution_bitcast_fusion.8), dimensions={2} | reverse | bytes 4194304 | tf_op jit(solution)/shard_map/rev | solution.py:39
  223.1 17.7 %rev.68 = f32[8,256,256]{2,1,0:T(8,128)} reverse(f32[8,256,256]{2,1,0:T(8,128)} %convolution_bitcast_fusion.7), dimensions={2} | reverse | bytes 4194304 | tf_op jit(solution)/shard_map/rev | solution.py:39
  242.6 17.7 %rev.69 = f32[8,256,256]{2,1,0:T(8,128)} reverse(f32[8,256,256]{2,1,0:T(8,128)} %convolution_bitcast_fusion.6), dimensions={2} | reverse | bytes 4194304 | tf_op jit(solution)/shard_map/rev | solution.py:39
  262.2 17.7 %rev.70 = f32[8,256,256]{2,1,0:T(8,128)} reverse(f32[8,256,256]{2,1,0:T(8,128)} %convolution_bitcast_fusion.5), dimensions={2} | reverse | bytes 4194304 | tf_op jit(solution)/shard_map/rev | solution.py:39
  281.7 17.6 %rev.71 = f32[8,256,256]{2,1,0:T(8,128)} reverse(f32[8,256,256]{2,1,0:T(8,128)} %convolution_bitcast_fusion.4), dimensions={2} | reverse | bytes 4194304 | tf_op jit(solution)/shard_map/rev | solution.py:39
  299.8 11.6 %rev.72 = f32[8,256,256]{2,1,0:T(8,128)} reverse(f32[8,256,256]{2,1,0:T(8,128)S(1)} %convolution_bitcast_fusion.14), dimensions={2} | reverse | bytes 4194304 | tf_op jit(solution)/shard_map/rev | solution.py:39
  313.2 11.6 %rev.73 = f32[8,256,256]{2,1,0:T(8,128)} reverse(f32[8,256,256]{2,1,0:T(8,128)S(1)} %convolution_bitcast_fusion.3), dimensions={2} | reverse | bytes 4194304 | tf_op jit(solution)/shard_map/rev | solution.py:39
  325.3 11.6 %rev.74 = f32[8,256,256]{2,1,0:T(8,128)} reverse(f32[8,256,256]{2,1,0:T(8,128)S(1)} %convolution_bitcast_fusion.2), dimensions={2} | reverse | bytes 4194304 | tf_op jit(solution)/shard_map/rev | solution.py:39
  337.5 11.6 %rev.75 = f32[8,256,256]{2,1,0:T(8,128)} reverse(f32[8,256,256]{2,1,0:T(8,128)S(1)} %convolution_bitcast_fusion.1), dimensions={2} | reverse | bytes 4194304 | tf_op jit(solution)/shard_map/rev | solution.py:39
  349.6 11.6 %rev.76 = f32[8,256,256]{2,1,0:T(8,128)} reverse(f32[8,256,256]{2,1,0:T(8,128)S(1)} %convolution_bitcast_fusion.13), dimensions={2} | reverse | bytes 4194304 | tf_op jit(solution)/shard_map/rev | solution.py:39
  361.8 11.7 %rev.77 = f32[8,256,256]{2,1,0:T(8,128)} reverse(f32[8,256,256]{2,1,0:T(8,128)S(1)} %convolution_bitcast_fusion.12), dimensions={2} | reverse | bytes 4194304 | tf_op jit(solution)/shard_map/rev | solution.py:39
  373.9 11.7 %rev.78 = f32[8,256,256]{2,1,0:T(8,128)} reverse(f32[8,256,256]{2,1,0:T(8,128)S(1)} %convolution_bitcast_fusion), dimensions={2} | reverse | bytes 4194304 | tf_op jit(solution)/shard_map/rev | solution.py:39
  386.1 11.8 %rev.79 = f32[8,256,256]{2,1,0:T(8,128)} reverse(f32[8,256,256]{2,1,0:T(8,128)S(1)} %fusion.81), dimensions={2} | reverse | bytes 4194304 | tf_op jit(solution)/shard_map/rev | solution.py:39
  402.2 7.0 reshape.447
  409.2 4.5 slice.1018
  419.3 7.0 reshape.445
  436.5 7.0 reshape.443
  443.5 4.5 slice.1014
  453.6 7.2 reshape.441
  460.8 4.5 slice.1012
  470.9 7.0 reshape.439
  488.1 7.0 reshape.437
  495.1 4.5 slice.1008
  505.2 7.4 reshape.435
  522.7 7.0 reshape.433
  539.8 7.0 reshape.431
  557.0 7.0 reshape.429
  574.3 7.0 reshape.427
  591.4 7.0 reshape.425
  608.5 7.0 reshape.423
  625.6 7.2 reshape.421
  643.0 7.0 reshape.417
  660.1 7.0 reshape.419
  683.2 5.2 collective-permute-done.1
  688.4 6.5 collective-permute-start.2
  714.0 5.1 reshape.407
  727.3 5.3 reshape.406
  740.9 5.1 reshape.405
  754.4 5.2 reshape.404
  770.3 5.0 reshape.403
  787.6 5.0 reshape.402
  804.7 5.2 reshape.401
  822.0 5.0 reshape.400
  839.4 5.2 reshape.415
  855.5 5.0 reshape.413
  871.7 5.4 reshape.412
  888.4 5.0 reshape.411
  905.0 5.2 reshape.410
  921.0 5.0 reshape.409
  935.8 5.2 reshape.408
  950.1 5.0 reshape.399
  955.2 7.7 fusion.36
  975.0 5.8 fusion.35
  990.8 25.6 %all_to_all.81 = bf16[32,128,128]{2,1,0:T(8,128)(2,1)S(1)} all-to-all(bf16[32,128,128]{2,1,0:T(8,128)(2,1)S(1)} %get-tuple-element.60), channel_id=1, replica_groups=mesh['dp'=8,'ctx'=32] {'ctx'}, dimensions={0} | all-to-all | bytes 2097152 | tf_op jit(solution)/shard_map/all_to_all | solution.py:124
  1016.4 20.7 %all_to_all.82 = bf16[32,128,128]{2,1,0:T(8,128)(2,1)S(1)} all-to-all(bf16[32,128,128]{2,1,0:T(8,128)(2,1)S(1)} %get-tuple-element.61), channel_id=1, replica_groups=mesh['dp'=8,'ctx'=32] {'ctx'}, dimensions={0} | all-to-all | bytes 2097152 | tf_op jit(solution)/shard_map/all_to_all | solution.py:123
  1046.6 11.7 %all-to-all-done.5 = bf16[32,128,128]{2,1,0:T(8,128)(2,1)S(1)} async-done(((bf16[32,128,128]{2,1,0:T(8,128)(2,1)}), bf16[32,128,128]{2,1,0:T(8,128)(2,1)S(1)}, u32[]{:S(2)}, u32[]{:S(2)}) %all-to-all-start.5) | async-done | bytes 1048608 | tf_op jit(solution)/shard_map/all_to_all | solution.py:125
  (584 shorter events, 480.4 us)
Async XLA Ops:
  4.7 8.7 copy-start.74
  4.7 25.9 %all-to-all-start.1 = ((bf16[128,32,128]{2,0,1:T(8,128)(2,1)}), bf16[128,32,128]{2,0,1:T(8,128)(2,1)S(1)}, u32[]{:S(2)}, u32[]{:S(2)}) async-start(bf16[128,32,128]{2,0,1:T(8,128)(2,1)} %copy.207), calls=%async_computation.1 | async-start | bytes 2097152 | tf_op jit(solution)/shard_map/all_to_all | solution.py:109
  30.6 21.3 %all-to-all-start = ((bf16[128,32,128]{2,0,1:T(8,128)(2,1)}), bf16[128,32,128]{2,0,1:T(8,128)(2,1)S(1)}, u32[]{:S(2)}, u32[]{:S(2)}) async-start(bf16[128,32,128]{2,0,1:T(8,128)(2,1)} %copy.204), calls=%async_computation | async-start | bytes 2097152 | tf_op jit(solution)/shard_map/all_to_all | solution.py:110
  36.2 20.7 %copy-start.82 = (s32[32]{0:T(128)S(1)}, s32[32]{0:T(128)}, u32[]{:S(2)}) copy-start(s32[32]{0:T(128)} %param.13) | copy-start | bytes 388
  51.9 22.2 %all-to-all-start.3 = ((bf16[128,32,128]{2,0,1:T(8,128)(2,1)}), bf16[128,32,128]{2,0,1:T(8,128)(2,1)}, u32[]{:S(2)}, u32[]{:S(2)}) async-start(bf16[128,32,128]{2,0,1:T(8,128)(2,1)} %copy.243), calls=%async_computation.3 | async-start | bytes 2097152 | tf_op jit(solution)/shard_map/all_to_all | solution.py:111
  57.0 19.0 %copy-start.79 = (pred[32]{0:T(512)(128)(4,1)}, pred[32]{0:T(512)(128)(4,1)S(1)}, u32[]{:S(2)}) copy-start(pred[32]{0:T(512)(128)(4,1)S(1)} %compare_and_fusion.1) | copy-start | bytes 100
  61.4 15.3 %copy-start.2 = (bf16[32,128,128]{2,1,0:T(8,128)(2,1)}, bf16[32,128,128]{2,1,0:T(8,128)(2,1)S(1)}, u32[]{:S(2)}) copy-start(bf16[32,128,128]{2,1,0:T(8,128)(2,1)S(1)} %gather_fusion) | copy-start | bytes 3145732
  77.6 4.3 slice-start.4
  79.5 306.0 %copy-start.75 = (bf16[256,8,16]{0,2,1:T(8,128)(2,1)}, bf16[256,8,16]{0,2,1:T(8,128)(2,1)S(1)}, u32[]{:S(2)}) copy-start(bf16[256,8,16]{0,2,1:T(8,128)(2,1)S(1)} %reshape.414) | copy-start | bytes 196612
  80.8 280.4 %copy-start.60 = (bf16[3,256,8,16]{1,0,3,2:T(4,128)(2,1)}, bf16[3,256,8,16]{1,0,3,2:T(4,128)(2,1)S(1)}, u32[]{:S(2)}) copy-start(bf16[3,256,8,16]{1,0,3,2:T(4,128)(2,1)S(1)} %slice.794) | copy-start | bytes 589828
  99.8 62.9 %copy-start.31 = (bf16[16,256,8,16]{1,0,3,2:T(8,128)(2,1)}, bf16[16,256,8,16]{1,0,3,2:T(8,128)(2,1)S(1)}, u32[]{:S(2)}) copy-start(bf16[16,256,8,16]{1,0,3,2:T(8,128)(2,1)S(1)} %reshape_reshape.4) | copy-start | bytes 3145732
  99.8 4.7 slice-start.15
  99.8 5.5 slice-start.16
  99.8 6.4 slice-start.17
  101.8 5.5 slice-start.18
  101.8 6.6 slice-start.19
  105.4 4.4 slice-start.20
  109.8 4.6 slice-start.22
  111.2 4.6 slice-start.23
  114.8 4.5 slice-start.24
  117.1 3.9 slice-start.25
  127.8 4.2 slice-start.28
  133.8 3.7 slice-start.29
  137.5 25.2 %copy-start.32 = (bf16[16,256,8,16]{1,0,3,2:T(8,128)(2,1)}, bf16[16,256,8,16]{1,0,3,2:T(8,128)(2,1)S(1)}, u32[]{:S(2)}) copy-start(bf16[16,256,8,16]{1,0,3,2:T(8,128)(2,1)S(1)} %convert_element_type.227) | copy-start | bytes 3145732
  164.5 17.7 %copy-start.35 = (bf16[14,256,8,16]{1,0,3,2:T(8,128)(2,1)S(1)}, bf16[14,256,8,16]{1,0,3,2:T(8,128)(2,1)}, u32[]{:S(2)}) copy-start(bf16[14,256,8,16]{1,0,3,2:T(8,128)(2,1)} %slice.695) | copy-start | bytes 2752516
  164.5 17.7 %copy-start.37 = (bf16[14,256,8,16]{1,0,3,2:T(8,128)(2,1)S(1)}, bf16[14,256,8,16]{1,0,3,2:T(8,128)(2,1)}, u32[]{:S(2)}) copy-start(bf16[14,256,8,16]{1,0,3,2:T(8,128)(2,1)} %slice.822) | copy-start | bytes 2752516
  184.0 17.7 %copy-start.38 = (bf16[13,256,8,16]{1,0,3,2:T(8,128)(2,1)S(1)}, bf16[13,256,8,16]{1,0,3,2:T(8,128)(2,1)}, u32[]{:S(2)}) copy-start(bf16[13,256,8,16]{1,0,3,2:T(8,128)(2,1)} %slice.704) | copy-start | bytes 2555908
  184.0 17.7 %copy-start.40 = (bf16[13,256,8,16]{1,0,3,2:T(8,128)(2,1)S(1)}, bf16[13,256,8,16]{1,0,3,2:T(8,128)(2,1)}, u32[]{:S(2)}) copy-start(bf16[13,256,8,16]{1,0,3,2:T(8,128)(2,1)} %slice.824) | copy-start | bytes 2555908
  203.5 17.7 %copy-start.41 = (bf16[12,256,8,16]{1,0,3,2:T(8,128)(2,1)S(1)}, bf16[12,256,8,16]{1,0,3,2:T(8,128)(2,1)}, u32[]{:S(2)}) copy-start(bf16[12,256,8,16]{1,0,3,2:T(8,128)(2,1)} %slice.713) | copy-start | bytes 2359300
  203.5 17.7 %copy-start.43 = (bf16[12,256,8,16]{1,0,3,2:T(8,128)(2,1)S(1)}, bf16[12,256,8,16]{1,0,3,2:T(8,128)(2,1)}, u32[]{:S(2)}) copy-start(bf16[12,256,8,16]{1,0,3,2:T(8,128)(2,1)} %slice.826) | copy-start | bytes 2359300
  223.1 17.7 %copy-start.44 = (bf16[11,256,8,16]{1,0,3,2:T(8,128)(2,1)S(1)}, bf16[11,256,8,16]{1,0,3,2:T(8,128)(2,1)}, u32[]{:S(2)}) copy-start(bf16[11,256,8,16]{1,0,3,2:T(8,128)(2,1)} %slice.722) | copy-start | bytes 2162692
  223.1 17.7 %copy-start.46 = (bf16[11,256,8,16]{1,0,3,2:T(8,128)(2,1)S(1)}, bf16[11,256,8,16]{1,0,3,2:T(8,128)(2,1)}, u32[]{:S(2)}) copy-start(bf16[11,256,8,16]{1,0,3,2:T(8,128)(2,1)} %slice.828) | copy-start | bytes 2162692
  242.6 17.7 %copy-start.47 = (bf16[10,256,8,16]{1,0,3,2:T(8,128)(2,1)S(1)}, bf16[10,256,8,16]{1,0,3,2:T(8,128)(2,1)}, u32[]{:S(2)}) copy-start(bf16[10,256,8,16]{1,0,3,2:T(8,128)(2,1)} %slice.731) | copy-start | bytes 1966084
  242.6 17.7 %copy-start.49 = (bf16[10,256,8,16]{1,0,3,2:T(8,128)(2,1)S(1)}, bf16[10,256,8,16]{1,0,3,2:T(8,128)(2,1)}, u32[]{:S(2)}) copy-start(bf16[10,256,8,16]{1,0,3,2:T(8,128)(2,1)} %slice.830) | copy-start | bytes 1966084
  262.2 17.7 %copy-start.51 = (bf16[9,256,8,16]{1,0,3,2:T(8,128)(2,1)S(1)}, bf16[9,256,8,16]{1,0,3,2:T(8,128)(2,1)}, u32[]{:S(2)}) copy-start(bf16[9,256,8,16]{1,0,3,2:T(8,128)(2,1)} %slice.740) | copy-start | bytes 1769476
  262.2 17.7 %copy-start.53 = (bf16[9,256,8,16]{1,0,3,2:T(8,128)(2,1)S(1)}, bf16[9,256,8,16]{1,0,3,2:T(8,128)(2,1)}, u32[]{:S(2)}) copy-start(bf16[9,256,8,16]{1,0,3,2:T(8,128)(2,1)} %slice.832) | copy-start | bytes 1769476
  281.7 17.6 %copy-start.55 = (bf16[8,256,8,16]{1,0,3,2:T(8,128)(2,1)S(1)}, bf16[8,256,8,16]{1,0,3,2:T(8,128)(2,1)}, u32[]{:S(2)}) copy-start(bf16[8,256,8,16]{1,0,3,2:T(8,128)(2,1)} %slice.749) | copy-start | bytes 1572868
  281.7 17.6 %copy-start.57 = (bf16[8,256,8,16]{1,0,3,2:T(8,128)(2,1)S(1)}, bf16[8,256,8,16]{1,0,3,2:T(8,128)(2,1)}, u32[]{:S(2)}) copy-start(bf16[8,256,8,16]{1,0,3,2:T(8,128)(2,1)} %slice.834) | copy-start | bytes 1572868
  313.2 11.7 %copy-start.62 = (bf16[6,256,8,16]{1,0,3,2:T(8,128)(2,1)S(1)}, bf16[6,256,8,16]{1,0,3,2:T(8,128)(2,1)}, u32[]{:S(2)}) copy-start(bf16[6,256,8,16]{1,0,3,2:T(8,128)(2,1)} %slice.767) | copy-start | bytes 1179652
  313.2 11.7 %copy-start.64 = (bf16[6,256,8,16]{1,0,3,2:T(8,128)(2,1)S(1)}, bf16[6,256,8,16]{1,0,3,2:T(8,128)(2,1)}, u32[]{:S(2)}) copy-start(bf16[6,256,8,16]{1,0,3,2:T(8,128)(2,1)} %slice.838) | copy-start | bytes 1179652
  325.3 11.6 %copy-start.66 = (bf16[5,256,8,16]{1,0,3,2:T(8,128)(2,1)S(1)}, bf16[5,256,8,16]{1,0,3,2:T(8,128)(2,1)}, u32[]{:S(2)}) copy-start(bf16[5,256,8,16]{1,0,3,2:T(8,128)(2,1)} %slice.776) | copy-start | bytes 983044
  325.3 11.6 %copy-start.68 = (bf16[5,256,8,16]{1,0,3,2:T(8,128)(2,1)S(1)}, bf16[5,256,8,16]{1,0,3,2:T(8,128)(2,1)}, u32[]{:S(2)}) copy-start(bf16[5,256,8,16]{1,0,3,2:T(8,128)(2,1)} %slice.840) | copy-start | bytes 983044
  337.5 11.7 %copy-start.71 = (bf16[4,256,8,16]{1,0,3,2:T(4,128)(2,1)S(1)}, bf16[4,256,8,16]{1,0,3,2:T(4,128)(2,1)}, u32[]{:S(2)}) copy-start(bf16[4,256,8,16]{1,0,3,2:T(4,128)(2,1)} %slice.785) | copy-start | bytes 786436
  337.5 11.6 %copy-start.72 = (bf16[4,256,8,16]{1,0,3,2:T(4,128)(2,1)S(1)}, bf16[4,256,8,16]{1,0,3,2:T(4,128)(2,1)}, u32[]{:S(2)}) copy-start(bf16[4,256,8,16]{1,0,3,2:T(4,128)(2,1)} %slice.842) | copy-start | bytes 786436
  349.6 11.6 %copy-start.61 = (bf16[3,256,8,16]{1,0,3,2:T(4,128)(2,1)S(1)}, bf16[3,256,8,16]{1,0,3,2:T(4,128)(2,1)}, u32[]{:S(2)}) copy-start(bf16[3,256,8,16]{1,0,3,2:T(4,128)(2,1)} %slice.844) | copy-start | bytes 589828
  361.7 11.7 %copy-start.69 = (bf16[2,256,8,16]{1,0,3,2:T(2,128)(2,1)S(1)}, bf16[2,256,8,16]{1,0,3,2:T(2,128)(2,1)}, u32[]{:S(2)}) copy-start(bf16[2,256,8,16]{1,0,3,2:T(2,128)(2,1)} %slice.803) | copy-start | bytes 393220
  361.8 11.7 %copy-start.70 = (bf16[2,256,8,16]{1,0,3,2:T(2,128)(2,1)S(1)}, bf16[2,256,8,16]{1,0,3,2:T(2,128)(2,1)}, u32[]{:S(2)}) copy-start(bf16[2,256,8,16]{1,0,3,2:T(2,128)(2,1)} %slice.846) | copy-start | bytes 393220
  373.9 11.7 %copy-start.76 = (bf16[256,8,16]{0,2,1:T(8,128)(2,1)S(1)}, bf16[256,8,16]{0,2,1:T(8,128)(2,1)}, u32[]{:S(2)}) copy-start(bf16[256,8,16]{0,2,1:T(8,128)(2,1)} %reshape.416) | copy-start | bytes 196612
  671.6 11.0 %copy-start.83 = (s32[32]{0:T(128)S(1)}, s32[32]{0:T(128)}, u32[]{:S(2)}) copy-start(s32[32]{0:T(128)} %param.13) | copy-start | bytes 388
  671.6 26.1 %copy-start.77 = (f32[8,4096]{1,0:T(8,128)S(1)}, f32[8,4096]{1,0:T(8,128)}, u32[]{:S(2)}) copy-start(f32[8,4096]{1,0:T(8,128)} %param.12) | copy-start | bytes 393220
  674.4 5.1 collective-permute-start
  679.6 8.9 collective-permute-start.1
  688.4 9.3 collective-permute-start.2
  714.0 5.1 copy-start.58
  727.3 5.3 copy-start.54
  740.9 5.1 copy-start.50
  941.0 3.7 copy-start.78
  955.1 7.7 copy-start.10
  971.2 3.8 copy-start.11
  971.2 3.8 copy-start.27
  971.2 3.8 copy-start.28
  971.2 3.8 copy-start.65
  984.4 3.9 copy-start.81
  1037.1 21.3 %all-to-all-start.5 = ((bf16[32,128,128]{2,1,0:T(8,128)(2,1)}), bf16[32,128,128]{2,1,0:T(8,128)(2,1)S(1)}, u32[]{:S(2)}, u32[]{:S(2)}) async-start(bf16[32,128,128]{2,1,0:T(8,128)(2,1)} %get-tuple-element.59), calls=%async_computation.5 | async-start | bytes 2097152 | tf_op jit(solution)/shard_map/all_to_all | solution.py:125
  (57 other events, 144.5 us)
